TPU v7x, 32 devices: a whole 2x2x4 slice. The times are simulated.
32 devices in a mesh: gx: 8 (over z, x), st: 4 (over y, core).
Axes of the slice: x: 2, y: 2, z: 4, core: 2. Of those that a mesh axis runs over, the one named last changes fastest.
Arguments:
- checkpoint: float32 [26, 64, 32, 128], P(None, ('gx', 'st')), may hold values from -0.5 to 1, as said below
- adjoint_in: float32 [26, 64, 32, 128], P(None, 'gx', 'st'), may hold values from -6 to 6
- solid_mask: int32 [64, 32, 128], P('gx', 'st'), may hold values 0 or 1
- tile_map: int32 [64, 32], P('gx', 'st'), may hold values from 0 to 4095
- theta: float32 [4096], replicated, may hold values from 0.8 to 1.2
- first_moment: float32 [4096], replicated, may hold values from -6 to 6
- second_moment: float32 [4096], replicated, may hold values from 1 to 30
Outputs:
- adjoint_out: float32 [26, 64, 32, 128], P(None, 'gx', 'st')
- theta_new: float32 [4096], replicated
- first_new: float32 [4096], replicated
- second_new: float32 [4096], replicated
- nusselt: float32 [], replicated
Inputs may be any that keep to these rules, and one draw needn't show every extreme that they name: `checkpoint`: populations near a local equilibrium; the flow populations of a cell sum to a density near 1.
All inputs are finite; a program needn't handle non-finite values. No bound on the sum of `solid_mask` on one device may be relied on, other than what follows from the above.
Results may differ from a plain program's by a relative error of at most 0.0001.
Values sent between devices are 32-bit elements; how exact they have to be, the bound alone decides.
A program may use at most 64 MiB of HBM per device.

v0:
```python
import functools

import jax
import jax.numpy as jnp
import numpy as np
from jax import lax
from jax.experimental import pallas as pl
from jax.experimental.pallas import tpu as pltpu
from jax.sharding import PartitionSpec as P

STEPS = 4
ADAM_STEP = 100

VELOCITY = [
    (0, 0, 0), (1, 0, 0), (-1, 0, 0), (0, 1, 0), (0, -1, 0), (0, 0, 1), (0, 0, -1),
    (1, 1, 0), (-1, -1, 0), (1, -1, 0), (-1, 1, 0), (1, 0, 1), (-1, 0, -1), (1, 0, -1),
    (-1, 0, 1), (0, 1, 1), (0, -1, -1), (0, 1, -1), (0, -1, 1),
    (0, 0, 0), (1, 0, 0), (-1, 0, 0), (0, 1, 0), (0, -1, 0), (0, 0, 1), (0, 0, -1),
]
WEIGHTS = [1.0 / 3.0] + [1.0 / 18.0] * 6 + [1.0 / 36.0] * 12 + [0.25] + [0.125] * 6
OPPOSITE = [0, 2, 1, 4, 3, 6, 5, 8, 7, 10, 9, 12, 11, 14, 13, 16, 15, 18, 17,
            19, 21, 20, 23, 22, 25, 24]
OMEGA = 1.25
LIFT = 0.8 * 0.001
MEAN_TEMP = 0.5
KAPPA = 0.075
RISING = 24
LEARN_RATE = 0.05
BETA_ONE = 0.9
BETA_TWO = 0.99
ADAM_EPS = 1e-08
MESH = pl.DeviceIdType.MESH

X_UP = [i for i in range(26) if VELOCITY[i][0] == 1]
X_DOWN = [i for i in range(26) if VELOCITY[i][0] == -1]
Y_UP = [i for i in range(26) if VELOCITY[i][1] == 1]
Y_DOWN = [i for i in range(26) if VELOCITY[i][1] == -1]
FAR = [(1, 0, 0, 6), (-1, 0, 6, 6), (1, 1, 12, 1), (-1, -1, 13, 1), (1, -1, 14, 1), (-1, 1, 15, 1)]
INNER = [(0, 1, 16, 6), (0, -1, 22, 6)]
EDGE = [(0, 1, 28, 6), (0, -1, 34, 6)]
GROUPS = [(FAR, 0, 16), (INNER, 16, 12), (EDGE, 28, 12)]
SINGLE = [(1, 0, 0, 1), (-1, 0, 1, 1), (0, 1, 2, 1), (0, -1, 3, 1),
          (1, 1, 4, 1), (-1, -1, 5, 1), (1, -1, 6, 1), (-1, 1, 7, 1)]
FACES = [(1, 0, 0, 2), (-1, 0, 2, 2), (0, 1, 4, 2), (0, -1, 6, 2)]
ROUND_ADJ = STEPS
ROUNDS = 2 * STEPS


def same(i):
    return i


def opposite(i):
    return OPPOSITE[i]


def kernel(n_gx, n_st, planes,
           check_ref, adj_ref, solid_hbm, map_hbm, theta_hbm, first_hbm, second_hbm,
           out_ref, theta_out, first_out, second_out, nu_out,
           solid_ref, map_ref, theta_ref, first_ref, second_ref, lam, nu, theta_new, first_new, second_new, start, adj, pops, rims, moments, table, plate,
           msg_out, msg_in, flag_out, flag_in, seed_out, seed_in, seed,
           mask_x, mask_lo, mask_hi, tiles, heat, grads, low_hot, high_hot,
           msg_sent, msg_got, flag_sent, flag_got, seed_sent, seed_got,
           all_sent, all_got, check_sent, check_got, own_sem, adj_sem, small_sem, out_sem):
    bx, by, nz = solid_ref.shape
    gx = lax.axis_index("gx")
    st = lax.axis_index("st")
    n = n_gx * n_st
    me = gx * n_st + st
    sub = lax.broadcasted_iota(jnp.int32, (by, nz), 0)
    lane = lax.broadcasted_iota(jnp.int32, (by, nz), 1)

    own = pltpu.make_async_copy(
        check_ref.at[:, :, pl.ds(pl.multiple_of(st * by, by), by), :],
        start.at[:, pl.ds(st * planes, planes)], own_sem)
    own.start()
    adj_copy = pltpu.make_async_copy(adj_ref, adj, adj_sem)
    adj_copy.start()
    small = [pltpu.make_async_copy(source, into, small_sem.at[k]) for k, (source, into) in enumerate(
        ((solid_hbm, solid_ref), (map_hbm, map_ref), (theta_hbm, theta_ref),
         (first_hbm, first_ref), (second_hbm, second_ref)))]
    for copy in small:
        copy.start()

    def device(offset):
        other = lax.rem(me + offset, n)
        return (other // n_st, lax.rem(other, n_st))

    barrier = pltpu.get_barrier_semaphore()

    @pl.loop(1, n)
    def _(offset):
        pl.semaphore_signal(barrier, inc=1, device_id=device(offset), device_id_type=MESH)

    pl.semaphore_wait(barrier, n - 1)

    def check_copy(step):
        other = lax.rem(st + step, n_st)
        return pltpu.make_async_remote_copy(
            src_ref=check_ref.at[:, :, pl.ds(pl.multiple_of(other * by, by), by), :],
            dst_ref=start.at[:, pl.ds(st * planes, planes)],
            send_sem=check_sent, recv_sem=check_got,
            device_id=(gx, other), device_id_type=MESH)

    for step in range(1, n_st):
        check_copy(step).start()

    def send(messages, out, into, sent, got):
        for dx, dy, first, count in messages:
            pltpu.make_async_remote_copy(
                src_ref=out.at[pl.ds(first, count)], dst_ref=into.at[pl.ds(first, count)],
                send_sem=sent, recv_sem=got,
                device_id=(lax.rem(gx + dx + n_gx, n_gx), lax.rem(st + dy + n_st, n_st)),
                device_id_type=MESH).start()

    def send_all(buf, k):
        @pl.loop(1, n)
        def _(offset):
            pltpu.make_async_remote_copy(
                src_ref=buf.at[0], dst_ref=buf.at[offset],
                send_sem=all_sent.at[k], recv_sem=all_got.at[k],
                device_id=device(offset), device_id_type=MESH).start()

    def wait_for(ref, sem):
        pltpu.make_async_copy(ref, ref, sem).wait()

    for copy in small:
        copy.wait()

    def flags(x, carry):
        value = solid_ref[x].astype(jnp.float32)
        mask_x[x + 1] = value
        flag_out[2, pl.ds(x, 1), :] = value[by - 1:by]
        flag_out[3, pl.ds(x, 1), :] = value[0:1]
        return carry

    lax.fori_loop(0, bx, flags, 0)
    flag_out[0] = mask_x[bx]
    flag_out[1] = mask_x[1]
    flag_out[4] = mask_x[bx]
    flag_out[5] = mask_x[1]
    flag_out[6] = mask_x[bx]
    flag_out[7] = mask_x[1]
    send(SINGLE, flag_out, flag_in, flag_sent, flag_got)

    cell_x = lax.broadcasted_iota(jnp.int32, (bx, nz), 0)
    cell_lane = lax.broadcasted_iota(jnp.int32, (bx, nz), 1)
    numbers = map_ref[...].astype(jnp.float32)
    row = jnp.zeros((bx, nz), jnp.float32)
    for y in range(by):
        row = row + jnp.where(cell_lane == bx * y + cell_x, numbers[:, y:y + 1] + 1.0, 0.0)
    tiles[0] = jnp.sum(row, 0, keepdims=True)
    send_all(tiles, 0)

    def joined(buf, pair):
        return buf[2 * pair] + pltpu.roll(buf[2 * pair + 1], nz // 2, 1)

    def hot(number):
        number = number - 1.0
        high = jnp.floor(number * (1.0 / nz))
        low = number - high * nz
        rows = theta_ref.shape[0]
        high_eq = lax.broadcasted_iota(jnp.int32, (rows, nz), 0).astype(jnp.float32) == high
        low_eq = lax.broadcasted_iota(jnp.int32, (nz, nz), 0).astype(jnp.float32) == low
        return jnp.where(high_eq, 1.0, 0.0), jnp.where(low_eq, 1.0, 0.0)

    def split(value):
        one = value.astype(jnp.bfloat16)
        rest = value - one.astype(jnp.float32)
        two = rest.astype(jnp.bfloat16)
        three = (rest - two.astype(jnp.float32)).astype(jnp.bfloat16)
        return jnp.concatenate([one, two, three], 0)

    def add_up(value):
        third = value.shape[0] // 3
        return value[:third] + value[third:2 * third] + value[2 * third:]

    high, low = hot(tiles[0])
    picked = lax.dot_general(split(theta_ref[...]), low.astype(jnp.bfloat16), (((1,), (0,)), ((), ())),
                             preferred_element_type=jnp.float32)
    temperature = jnp.sum(add_up(picked) * high, 0, keepdims=True)

    def lay_plate(x, carry):
        chosen = jnp.where(lane == bx * sub + x, temperature, 0.0)
        total = jnp.sum(chosen, 1, keepdims=True)
        plate[x] = jnp.where(lane == 0, 0.25 * total, 0.0)
        return carry

    lax.fori_loop(0, bx, lay_plate, 0)

    def pack_rows(r, which, values, x, base):
        for k, i in enumerate(Y_UP):
            msg_out[r, base + k, pl.ds(x, 1), :] = values(which(i))[by - 1:by]
        for k, i in enumerate(Y_DOWN):
            msg_out[r, base + 6 + k, pl.ds(x, 1), :] = values(which(i))[0:1]

    def pack_planes(r, which, last, first):
        for k, i in enumerate(X_UP):
            msg_out[r, k] = last(which(i))
        for k, i in enumerate(X_DOWN):
            msg_out[r, 6 + k] = first(which(i))
        msg_out[r, 12] = last(which(7))
        msg_out[r, 13] = first(which(8))
        msg_out[r, 14] = last(which(9))
        msg_out[r, 15] = first(which(10))

    def send_group(r, group):
        send(GROUPS[group][0], msg_out.at[r], msg_in.at[r], msg_sent.at[r], msg_got.at[r, group])

    def wait_group(r, group):
        _, first, count = GROUPS[group]
        wait_for(msg_in.at[r, pl.ds(first, count)], msg_got.at[r, group])

    def unpack_far(r, which, pop, rim, extra=None):
        def arrived(slot, i, side):
            value = msg_in[r, slot]
            return value if extra is None else value + extra(which(i), side)

        for k, i in enumerate(X_UP):
            pop[which(i), 0] = arrived(k, i, 0)
        for k, i in enumerate(X_DOWN):
            pop[which(i), bx + 1] = arrived(6 + k, i, 1)
        rim[which(7), 0:1, :] = msg_in[r, 12, by - 1:by, :]
        rim[which(8), bx + 1:bx + 2, :] = msg_in[r, 13, 0:1, :]
        rim[which(9), 0:1, :] = msg_in[r, 14, 0:1, :]
        rim[which(10), bx + 1:bx + 2, :] = msg_in[r, 15, by - 1:by, :]

    def unpack_inner(r, which, rim, extra=None):
        for side, rows_of, base in ((2, Y_UP, 16), (3, Y_DOWN, 22)):
            for k, i in enumerate(rows_of):
                value = msg_in[r, base + k]
                if extra is not None:
                    value = value + extra(which(i), side)
                rim[which(i), 2:bx, :] = value[1:bx - 1]

    def unpack_edge(r, which, rim, extra=None):
        for side, rows_of, base in ((2, Y_UP, 28), (3, Y_DOWN, 34)):
            for k, i in enumerate(rows_of):
                value = msg_in[r, base + k]
                if extra is not None:
                    value = value + extra(which(i), side)
                rim[which(i), 1:2, :] = value[0:1]
                rim[which(i), bx:bx + 1, :] = value[bx - 1:bx]

    def turn(value, edge, step_y, step_z):
        if step_y == 1:
            value = jnp.where(sub == 0, edge, pltpu.roll(value, 1, 0))
        elif step_y == -1:
            value = jnp.where(sub == by - 1, edge, pltpu.roll(value, by - 1, 0))
        if step_z == 1:
            value = pltpu.roll(value, 1, 1)
        elif step_z == -1:
            value = pltpu.roll(value, nz - 1, 1)
        return value

    def pull(pop, rim, source, i, x):
        step_x, step_y, step_z = VELOCITY[i]
        edge = rim[source, pl.ds(x + 1 - step_x, 1), :] if step_y else None
        return turn(pop[source, x + 1 - step_x], edge, step_y, step_z)

    wait_for(flag_in, flag_got)
    mask_x[0] = flag_in[0]
    mask_x[bx + 1] = flag_in[1]
    mask_lo[1:bx + 1, :] = flag_in[2]
    mask_hi[1:bx + 1, :] = flag_in[3]
    mask_lo[0:1, :] = flag_in[4, by - 1:by, :]
    mask_hi[bx + 1:bx + 2, :] = flag_in[5, 0:1, :]
    mask_hi[0:1, :] = flag_in[6, 0:1, :]
    mask_lo[bx + 1:bx + 2, :] = flag_in[7, by - 1:by, :]

    def fill_table(x, carry):
        for i in range(1, 19):
            step_x, step_y, step_z = VELOCITY[i]
            edge = None
            if step_y:
                edge = (mask_lo if step_y == 1 else mask_hi)[pl.ds(x + 1 - step_x, 1), :]
            value = turn(mask_x[x + 1 - step_x], edge, step_y, step_z)
            if step_z:
                value = jnp.where(lane == (0 if step_z == 1 else nz - 1), 1.0, value)
            table[i, x] = value
        return carry

    lax.fori_loop(0, bx, fill_table, 0)

    def moments_of(s):
        def pairs(i):
            return s[i] + s[i + 1], s[i] - s[i + 1]

        p = {}
        m = {}
        for i in range(1, 19, 2):
            p[i], m[i] = pairs(i)
        density = s[0] + ((p[1] + p[3]) + (p[5] + p[7])) + ((p[9] + p[11]) + (p[13] + p[15])) + p[17]
        speed_x = (m[1] + m[7]) + (m[9] + m[11]) + m[13]
        speed_y = (m[3] + m[7]) + (m[15] + m[17]) - m[9]
        speed_z = (m[5] + m[11]) + (m[15] - m[17]) - m[13]
        temper = (s[19] + s[20]) + (s[21] + s[22]) + (s[23] + s[24]) + s[25]
        return density, speed_x, speed_y, speed_z, temper

    def along(c, a, b, d):
        total = None
        for step, value in zip(c, (a, b, d)):
            if step == 0:
                continue
            if total is None:
                total = value if step == 1 else -value
            else:
                total = total + value if step == 1 else total - value
        return total

    def collide(s):
        density, ux, uy, uz, temper = moments_of(s)
        vz = uz + LIFT * (temper - MEAN_TEMP)
        base = density - 1.5 * (ux * ux + uy * uy + vz * vz)
        post = [None] * 26
        post[0] = (1.0 - OMEGA) * s[0] + (OMEGA * WEIGHTS[0]) * base
        for i in range(1, 19, 2):
            cv = along(VELOCITY[i], ux, uy, vz)
            even = base + (4.5 * cv) * cv
            odd = 3.0 * cv
            weight = OMEGA * WEIGHTS[i]
            post[i] = (1.0 - OMEGA) * s[i] + weight * (even + odd)
            post[i + 1] = (1.0 - OMEGA) * s[i + 1] + weight * (even - odd)
        post[19] = (1.0 - OMEGA) * s[19] + (OMEGA * WEIGHTS[19]) * temper
        share = (OMEGA * WEIGHTS[20]) * temper
        for i, u in ((20, ux), (22, uy), (24, uz)):
            odd = (4.0 * u) * share
            post[i] = (1.0 - OMEGA) * s[i] + (share + odd)
            post[i + 1] = (1.0 - OMEGA) * s[i + 1] + (share - odd)
        return post, (ux, uy, uz, temper)

    def keep(pop, r, which, values, x, base):
        for i in range(26):
            pop[i, x + 1] = values[i]
        pack_rows(r, which, lambda j: values[j], x, base)

    def ship_edges(pop, r, which):
        pack_planes(r, which, lambda j: pop[j, bx], lambda j: pop[j, 1])
        send_group(r, 0)
        send_group(r, 2)

    def remember(k, x, values):
        for part in range(4):
            moments[k, part, x] = values[part]

    inner_pairs = (bx - 4) // 2
    pairs_x = bx // 2

    def place(it):
        inner = it < inner_pairs
        away = pairs_x - 1 - it
        return (jnp.where(inner, 2 + 2 * it, away),
                jnp.where(inner, 3 + 2 * it, bx - 1 - away))

    def whole_step(work, carry, pop, r, which):
        carry = work(0, bx - 1, carry, 28)
        ship_edges(pop, r, which)
        carry = lax.fori_loop(
            0, pairs_x - 1, lambda it, c: work(1 + 2 * it, 2 + 2 * it, c, 16), carry)
        send_group(r, 1)
        return carry

    def fed_step(work, carry, old, rim, r, which, new=None, between=None):
        def pair(it, total):
            @pl.when(it == 0)
            def _():
                wait_group(r, 1)
                unpack_inner(r, which, rim)

            @pl.when(it == inner_pairs)
            def _():
                wait_group(r, 2)
                unpack_edge(r, which, rim)

            @pl.when(it == pairs_x - 1)
            def _():
                if new is not None:
                    send_group(r + 1, 1)
                if between is not None:
                    between()
                wait_group(r, 0)
                unpack_far(r, which, old, rim)

            first, second = place(it)
            return work(first, second, total, jnp.where(it == pairs_x - 1, 28, 16))

        carry = lax.fori_loop(0, pairs_x, pair, carry)
        if new is not None:
            ship_edges(new, r + 1, which)
        return carry

    def propagated(pop, rim, x):
        result = [pop[0, x + 1]] + [None] * 25
        result[19] = pop[19, x + 1]
        for i in range(1, 26):
            if i == 19:
                continue
            solid = table[i if i < 19 else i - 19, x] > 0.5
            back = pop[OPPOSITE[i], x + 1]
            if i == 24:
                back = jnp.where(lane == 0, -back, back)
            elif i == 25:
                back = jnp.where(lane == nz - 1, -back, back)
            result[i] = jnp.where(solid, back, pull(pop, rim, i, i, x))
        result[RISING] = result[RISING] + plate[x]
        return result

    wait_for(tiles.at[pl.ds(1, n - 1)], all_got.at[0])

    def fill_hot(pair, carry):
        high, low = hot(joined(tiles, pair))
        high_hot[pair] = high
        low_hot[pl.ds(pl.multiple_of(pair * nz, nz), nz), :] = low.T.astype(jnp.bfloat16)
        return carry

    lax.fori_loop(0, n // 2, fill_hot, 0)


    own.wait()
    wait_for(start.at[:, pl.ds(0, (n_st - 1) * planes)], check_got)

    def begin(first, second, carry, base):
        done = [collide([start[i, x] for i in range(26)]) for x in (first, second)]
        for x, (post, values) in zip((first, second), done):
            keep(pops.at[0], 0, same, post, x, base)
            remember(0, x, values)
        return carry

    whole_step(begin, 0, pops.at[0], 0, same)

    adj_copy.wait()

    def adj_rows(x, carry):
        pack_rows(ROUND_ADJ, opposite, lambda j: adj[j, x], x, 16)
        return carry

    lax.fori_loop(1, bx - 1, adj_rows, 0)
    for x in (0, bx - 1):
        pack_rows(ROUND_ADJ, opposite, lambda j, x=x: adj[j, x], x, 28)
    pack_planes(ROUND_ADJ, opposite, lambda j: adj[j, bx - 1], lambda j: adj[j, 0])
    for group in range(3):
        send_group(ROUND_ADJ, group)

    def forward(k, carry):
        now = lax.rem(k, 2)
        old, new, rim = pops.at[1 - now], pops.at[now], rims.at[1 - now]

        def advance(first, second, carry, base):
            done = [collide(propagated(old, rim, x)) for x in (first, second)]
            for x, (post, values) in zip((first, second), done):
                keep(new, k, same, post, x, base)
                remember(k, x, values)
            return carry

        return fed_step(advance, carry, old, rim, k - 1, same, new)

    lax.fori_loop(1, STEPS, forward, 0)

    last, rim = pops.at[(STEPS - 1) % 2], rims.at[(STEPS - 1) % 2]

    def finish(first, second, total, base):
        return finish_plane(second, finish_plane(first, total))

    def finish_plane(x, total):
        _, _, _, uz, temper = moments_of(propagated(last, rim, x))
        fluid = 1.0 - mask_x[x + 1]
        warm = fluid * temper
        rise = fluid * uz
        seed[0, x] = warm
        seed[1, x] = rise
        seed_out[4, pl.ds(x, 1), :] = warm[by - 1:by]
        seed_out[5, pl.ds(x, 1), :] = rise[by - 1:by]
        seed_out[6, pl.ds(x, 1), :] = warm[0:1]
        seed_out[7, pl.ds(x, 1), :] = rise[0:1]
        return total + warm * uz

    flux = fed_step(finish, jnp.zeros((by, nz), jnp.float32), last, rim, STEPS - 1, same)
    heat[0] = jnp.sum(flux, 0, keepdims=True)
    send_all(heat, 1)
    seed_out[0] = seed[0, bx - 1]
    seed_out[1] = seed[1, bx - 1]
    seed_out[2] = seed[0, 0]
    seed_out[3] = seed[1, 0]
    send(FACES, seed_out, seed_in, seed_sent, seed_got)
    for group in range(3):
        wait_group(ROUND_ADJ, group)
    wait_for(seed_in, seed_got)
    wait_for(heat.at[pl.ds(1, n - 1)], all_got.at[1])
    heat_sum = jnp.sum(jnp.sum(heat[...], 0), 1, keepdims=True)
    nusselt = 1.0 + heat_sum / (KAPPA * (bx * n_gx * by * n_st))
    nu[...] = nusselt
    gain = jnp.broadcast_to(nusselt - 1.0, (by, nz))

    def seeded(j, warm, rise):
        if j >= 19:
            return gain * rise
        if VELOCITY[j][2] == 0:
            return jnp.zeros((by, nz), jnp.float32)
        return gain * warm if VELOCITY[j][2] == 1 else -(gain * warm)

    def bed_of(value, x):
        return jnp.where(lane == bx * sub + x, 0.25 * value[:, 0:1], 0.0)

    def seed_adjoint(x, total):
        warm = seed[0, x]
        rise = seed[1, x]
        for j in range(26):
            value = adj[j, x] + seeded(j, warm, rise)
            pops[0, j, x + 1] = value
            if j == RISING:
                total = total + bed_of(value, x)
        return total

    total = lax.fori_loop(0, bx, seed_adjoint, jnp.zeros((by, nz), jnp.float32))

    def arrived_seed(j, side):
        return seeded(j, seed_in[2 * side], seed_in[2 * side + 1])

    unpack_far(ROUND_ADJ, opposite, pops.at[0], rims.at[0], arrived_seed)
    unpack_inner(ROUND_ADJ, opposite, rims.at[0], arrived_seed)
    unpack_edge(ROUND_ADJ, opposite, rims.at[0], arrived_seed)

    def pulled_back(pop, rim, x):
        fluid = 1.0 - mask_x[x + 1]
        above = jnp.where(lane == 0, 0.0, fluid)
        below = jnp.where(lane == nz - 1, 0.0, fluid)
        mu = [None] * 26
        mu[0] = pop[0, x + 1]
        mu[19] = pop[19, x + 1]
        for i in range(1, 26):
            if i == 19:
                continue
            step_z = VELOCITY[i][2]
            share = fluid if step_z == 0 else (above if step_z == 1 else below)
            bounce = table[i if i < 19 else i - 19, x]
            if i == 24:
                bounce = jnp.where(lane == 0, -1.0, bounce)
            elif i == 25:
                bounce = jnp.where(lane == nz - 1, -1.0, bounce)
            mu[OPPOSITE[i]] = share * pull(pop, rim, OPPOSITE[i], i, x) + bounce * pop[i, x + 1]
        return mu

    def collide_back(mu, k, x):
        ux = moments[k, 0, x]
        uy = moments[k, 1, x]
        uz = moments[k, 2, x]
        temper = moments[k, 3, x]
        vz = uz + LIFT * (temper - MEAN_TEMP)
        even = {}
        odd = {}
        for i in range(1, 19, 2):
            even[i] = mu[i] + mu[i + 1]
            odd[i] = mu[i] - mu[i + 1]
        axis = OMEGA * WEIGHTS[1]
        diag = OMEGA * WEIGHTS[7]
        xy = diag * (even[7] + even[9])
        xz = diag * (even[11] + even[13])
        yz = diag * (even[15] + even[17])
        ex, ey, ez = axis * even[1], axis * even[3], axis * even[5]
        zero = (OMEGA * WEIGHTS[0]) * mu[0] + ((ex + ey) + (ez + xy)) + (xz + yz)
        sxx = ex + (xy + xz)
        syy = ey + (xy + yz)
        szz = ez + (xz + yz)
        sxy = diag * (even[7] - even[9])
        sxz = diag * (even[11] - even[13])
        syz = diag * (even[15] - even[17])
        one_x = axis * odd[1] + diag * ((odd[7] + odd[9]) + (odd[11] + odd[13]))
        one_y = axis * odd[3] + diag * ((odd[7] - odd[9]) + (odd[15] + odd[17]))
        one_z = axis * odd[5] + diag * ((odd[11] - odd[13]) + (odd[15] - odd[17]))
        bar_x = 3.0 * (one_x - zero * ux) + 9.0 * (sxx * ux + sxy * uy + sxz * vz)
        bar_y = 3.0 * (one_y - zero * uy) + 9.0 * (sxy * ux + syy * uy + syz * vz)
        bar_z = 3.0 * (one_z - zero * vz) + 9.0 * (sxz * ux + syz * uy + szz * vz)
        share = OMEGA * WEIGHTS[20]
        hx = (4.0 * share) * (mu[20] - mu[21])
        hy = (4.0 * share) * (mu[22] - mu[23])
        hz = (4.0 * share) * (mu[24] - mu[25])
        warm = (OMEGA * WEIGHTS[19]) * mu[19] + share * (
            ((mu[20] + mu[21]) + (mu[22] + mu[23])) + (mu[24] + mu[25]))
        bar_t = warm + (hx * ux + hy * uy + hz * uz) + LIFT * bar_z
        bar_x = bar_x + temper * hx
        bar_y = bar_y + temper * hy
        bar_z = bar_z + temper * hz
        lam = [None] * 26
        lam[0] = (1.0 - OMEGA) * mu[0] + zero
        for i in range(1, 19, 2):
            cb = along(VELOCITY[i], bar_x, bar_y, bar_z)
            lam[i] = (1.0 - OMEGA) * mu[i] + (zero + cb)
            lam[i + 1] = (1.0 - OMEGA) * mu[i + 1] + (zero - cb)
        for i in range(19, 26):
            lam[i] = (1.0 - OMEGA) * mu[i] + bar_t
        return lam

    def backward(step, total, fed=True):
        now = lax.rem(step, 2)
        old, new, rim = pops.at[now], pops.at[1 - now], rims.at[now]
        k = STEPS - 1 - step
        r = ROUND_ADJ + step

        def retreat(first, second, total, base):
            done = [collide_back(pulled_back(old, rim, x), k, x) for x in (first, second)]
            for x, values in zip((first, second), done):
                keep(new, r + 1, opposite, values, x, base)
                total = total + bed_of(values[RISING], x)
            return total

        if fed:
            return fed_step(retreat, total, old, rim, r, opposite, new)
        return whole_step(retreat, total, new, r + 1, opposite)

    total = backward(0, total, False)
    total = lax.fori_loop(1, STEPS - 1, backward, total)

    grads[0] = jnp.sum(total, 0, keepdims=True)
    send_all(grads, 2)

    small_out = [pltpu.make_async_copy(source, into, out_sem.at[k]) for k, (source, into) in enumerate(
        ((theta_new, theta_out), (first_new, first_out), (second_new, second_out), (nu, nu_out)))]

    def inner_out():
        return pltpu.make_async_copy(lam.at[:, pl.ds(1, bx - 2)], out_ref.at[:, pl.ds(1, bx - 2)],
                                     out_sem.at[4])

    def edge_out(x, k):
        return pltpu.make_async_copy(lam.at[:, pl.ds(x, 1)], out_ref.at[:, pl.ds(x, 1)],
                                     out_sem.at[k])

    def update_tiles():
        inner_out().start()
        wait_for(grads.at[pl.ds(1, n - 1)], all_got.at[2])
        rows = theta_ref.shape[0]
        pairs = n // 2
        part = 16 if pairs % 16 == 0 else pairs

        def gather_tiles(chunk, total):
            weighted = [split(high_hot[chunk * part + p] * joined(grads, chunk * part + p))
                        for p in range(part)]
            low = low_hot[pl.ds(pl.multiple_of(chunk * (part * nz), nz), part * nz), :]
            return total + jnp.dot(jnp.concatenate(weighted, 1), low,
                                   preferred_element_type=jnp.float32)

        tile_grad = add_up(lax.fori_loop(0, pairs // part, gather_tiles,
                                            jnp.zeros((3 * rows, nz), jnp.float32)))
        first = BETA_ONE * first_ref[...] + (1.0 - BETA_ONE) * tile_grad
        second = BETA_TWO * second_ref[...] + (1.0 - BETA_TWO) * tile_grad * tile_grad
        first_hat = first / (1.0 - BETA_ONE**ADAM_STEP)
        second_hat = second / (1.0 - BETA_TWO**ADAM_STEP)
        first_new[...] = first
        second_new[...] = second
        theta_new[...] = theta_ref[...] - LEARN_RATE * first_hat / (jnp.sqrt(second_hat) + ADAM_EPS)
        for copy in small_out:
            copy.start()

    old, rim = pops.at[(STEPS - 1) % 2], rims.at[(STEPS - 1) % 2]

    def end(first, second, carry, base):
        done = [collide_back(pulled_back(old, rim, x), 0, x) for x in (first, second)]
        for x, values in zip((first, second), done):
            for i in range(26):
                lam[i, x] = values[i]
        return carry

    fed_step(end, 0, old, rim, ROUND_ADJ + STEPS - 1, opposite, between=update_tiles)
    edge_out(0, 5).start()
    edge_out(bx - 1, 6).start()

    wait_for(start.at[:, pl.ds(0, (n_st - 1) * planes)], check_sent)
    wait_for(flag_out, flag_sent)
    wait_for(seed_out, seed_sent)
    for r in range(ROUNDS):
        wait_for(msg_out.at[r], msg_sent.at[r])
    wait_for(tiles.at[pl.ds(1, n - 1)], all_sent.at[0])
    wait_for(heat.at[pl.ds(1, n - 1)], all_sent.at[1])
    wait_for(grads.at[pl.ds(1, n - 1)], all_sent.at[2])
    for copy in small_out:
        copy.wait()
    inner_out().wait()
    edge_out(0, 5).wait()
    edge_out(bx - 1, 6).wait()


def deliver(*refs):
    sem = refs[-1]
    half = (len(refs) - 1) // 2
    copies = [pltpu.make_async_copy(refs[k], refs[half + k], sem.at[k]) for k in range(half)]
    for copy in copies:
        copy.start()
    for copy in copies:
        copy.wait()


def body(n_gx, n_st, checkpoint, adjoint_in, solid_mask, tile_map, theta, first_moment, second_moment):
    bx, by, nz = solid_mask.shape
    planes = checkpoint.shape[1]
    n = n_gx * n_st
    rows = theta.shape[0] // nz
    f32 = jnp.float32
    wide = 16
    vmem = pl.BlockSpec(memory_space=pltpu.VMEM)
    hbm = pl.BlockSpec(memory_space=pltpu.HBM)
    dma = pltpu.SemaphoreType.DMA
    small = jax.ShapeDtypeStruct((rows, nz), f32)
    shapes = (jax.ShapeDtypeStruct((26, bx, by, nz), f32), small, small, small,
              jax.ShapeDtypeStruct((1, 1), f32))
    results = pl.pallas_call(
        functools.partial(kernel, n_gx, n_st, planes),
        out_shape=tuple(pltpu.HBM(value.shape, f32) for value in shapes),
        in_specs=[hbm] * 7,
        out_specs=(hbm,) * 5,
        scratch_shapes=[
            pltpu.VMEM((bx, by, nz), jnp.int32),
            pltpu.VMEM((bx, by), jnp.int32),
            pltpu.VMEM((rows, nz), f32),
            pltpu.VMEM((rows, nz), f32),
            pltpu.VMEM((rows, nz), f32),
            pltpu.VMEM((26, bx, by, nz), f32),
            pltpu.VMEM((1, 1), f32),
            pltpu.VMEM((rows, nz), f32),
            pltpu.VMEM((rows, nz), f32),
            pltpu.VMEM((rows, nz), f32),
            pltpu.VMEM((26, bx, by, nz), f32),
            pltpu.VMEM((26, bx, by, nz), f32),
            pltpu.VMEM((2, 26, bx + 2, by, nz), f32),
            pltpu.VMEM((2, 26, wide, nz), f32),
            pltpu.VMEM((STEPS, 4, bx, by, nz), f32),
            pltpu.VMEM((19, bx, by, nz), f32),
            pltpu.VMEM((bx, by, nz), f32),
            pltpu.VMEM((ROUNDS, 40, by, nz), f32),
            pltpu.VMEM((ROUNDS, 40, by, nz), f32),
            pltpu.VMEM((8, by, nz), f32),
            pltpu.VMEM((8, by, nz), f32),
            pltpu.VMEM((8, by, nz), f32),
            pltpu.VMEM((8, by, nz), f32),
            pltpu.VMEM((2, bx, by, nz), f32),
            pltpu.VMEM((bx + 2, by, nz), f32),
            pltpu.VMEM((wide, nz), f32),
            pltpu.VMEM((wide, nz), f32),
            pltpu.VMEM((n, 1, nz), f32),
            pltpu.VMEM((n, 1, nz), f32),
            pltpu.VMEM((n, 1, nz), f32),
            pltpu.VMEM((n // 2 * nz, nz), jnp.bfloat16),
            pltpu.VMEM((n // 2, rows, nz), f32),
            dma((ROUNDS,)),
            dma((ROUNDS, 3)),
            dma,
            dma,
            dma,
            dma,
            dma((3,)),
            dma((3,)),
            dma,
            dma,
            dma,
            dma,
            dma((5,)),
            dma((7,)),
        ],
        compiler_params=pltpu.CompilerParams(
            collective_id=0, has_side_effects=True, vmem_limit_bytes=40 * 1024 * 1024),
        name="window",
    )(*(pltpu.with_memory_space_constraint(value, pltpu.HBM) for value in (
        checkpoint, adjoint_in, solid_mask, tile_map, theta.reshape(rows, nz),
        first_moment.reshape(rows, nz), second_moment.reshape(rows, nz))))
    adjoint_out, theta_new, first_new, second_new, nusselt = pl.pallas_call(
        deliver,
        out_shape=shapes,
        in_specs=[hbm] * 5,
        out_specs=(hbm,) * 5,
        scratch_shapes=[dma((5,))],
        name="deliver",
    )(*(pltpu.with_memory_space_constraint(value, pltpu.HBM) for value in results))
    flat = theta.shape
    return (adjoint_out, theta_new.reshape(flat), first_new.reshape(flat),
            second_new.reshape(flat), nusselt.reshape(()))


def solution(mesh):
    return jax.shard_map(
        functools.partial(body, mesh.shape["gx"], mesh.shape["st"]),
        mesh=mesh,
        in_specs=(
            P(None, ("gx", "st"), None, None),
            P(None, "gx", "st", None),
            P("gx", "st", None),
            P("gx", "st"),
            P(),
            P(),
            P(),
        ),
        out_specs=(P(None, "gx", "st", None), P(), P(), P(), P()),
        check_vma=False,
    )
```

profile of v0, /device:TPU:0, one launch (start us, length us, event | category | flops | bytes accessed | tf_op | source)
XLA Modules:
  0.0 91.4 jit_solution(318070616979131157)
XLA Ops:
  0.6 61.6 %window.1 = (f32[26,8,8,128]{3,2,1,0:T(8,128)}, f32[32,128]{1,0:T(8,128)}, f32[32,128]{1,0:T(8,128)}, f32[32,128]{1,0:T(8,128)}, f32[1,1]{1,0:T(1,128)}) custom-call(f32[26,2,32,128]{3,2,1,0:T(8,128)} %check_ref.1, f32[26,8,8,128]{3,2,1,0:T(8,128)} %adj_ref.1, s32[8,8,128]{2,1,0:T(8,128)} %solid_hbm.1, s32[8,8]{1,0:T(8,128)} %map_hbm.1, f32[32,128]{1,0:T(8,128)} %bitcast.7, ...), custom_call_target="tpu_custom_call" | custom-call | tf_op jit(solution)/shard_map/window/pallas_call | solution.py:704
  62.3 29.1 %deliver.1 = (f32[26,8,8,128]{3,2,1,0:T(8,128)}, f32[32,128]{1,0:T(8,128)}, f32[32,128]{1,0:T(8,128)}, f32[32,128]{1,0:T(8,128)}, f32[1,1]{1,0:T(1,128)}) custom-call(f32[26,8,8,128]{3,2,1,0:T(8,128)} %get-tuple-element.15.refs_0_, f32[32,128]{1,0:T(8,128)} %get-tuple-element.16.refs_1_, f32[32,128]{1,0:T(8,128)} %get-tuple-element.17.refs_2_, ...), custom_call_target="tpu_custom_call" | custom-call | tf_op jit(solution)/shard_map/deliver/pallas_call | solution.py:763
where the time goes:
time: 91.5 us; the launch traced here: 91.4 us
  Pallas kernels  90.7 us (99%)
    pallas_call x1, Pallas kernels, body(): pl.pallas_call(functools.partial(kernel, n_gx, n_st, planes), out_shape=t...  61.6 us
    pallas_call x1, Pallas kernels, body(): pl.pallas_call(deliver, out_shape=shapes, in_specs=[hbm] * 5, out_specs=(...  29.1 us

commit v1 on v0

--- a/solution.py
+++ b/solution.py
@@ -56,12 +56,12 @@
 
 def kernel(n_gx, n_st, planes,
            check_ref, adj_ref, solid_hbm, map_hbm, theta_hbm, first_hbm, second_hbm,
-           out_ref, theta_out, first_out, second_out, nu_out,
-           solid_ref, map_ref, theta_ref, first_ref, second_ref, lam, nu, theta_new, first_new, second_new, start, adj, pops, rims, moments, table, plate,
+           lam, theta_new, first_new, second_new, nu,
+           solid_ref, map_ref, theta_ref, first_ref, second_ref, start, adj, pops, rims, moments, table, plate,
            msg_out, msg_in, flag_out, flag_in, seed_out, seed_in, seed,
            mask_x, mask_lo, mask_hi, tiles, heat, grads, low_hot, high_hot,
            msg_sent, msg_got, flag_sent, flag_got, seed_sent, seed_got,
-           all_sent, all_got, check_sent, check_got, own_sem, adj_sem, small_sem, out_sem):
+           all_sent, all_got, check_sent, check_got, own_sem, adj_sem, small_sem):
     bx, by, nz = solid_ref.shape
     gx = lax.axis_index("gx")
     st = lax.axis_index("st")
@@ -488,7 +488,7 @@
     wait_for(heat.at[pl.ds(1, n - 1)], all_got.at[1])
     heat_sum = jnp.sum(jnp.sum(heat[...], 0), 1, keepdims=True)
     nusselt = 1.0 + heat_sum / (KAPPA * (bx * n_gx * by * n_st))
-    nu[...] = nusselt
+    nu[...] = jnp.broadcast_to(nusselt, nu.shape)
     gain = jnp.broadcast_to(nusselt - 1.0, (by, nz))
 
     def seeded(j, warm, rise):
@@ -613,19 +613,7 @@
     grads[0] = jnp.sum(total, 0, keepdims=True)
     send_all(grads, 2)
 
-    small_out = [pltpu.make_async_copy(source, into, out_sem.at[k]) for k, (source, into) in enumerate(
-        ((theta_new, theta_out), (first_new, first_out), (second_new, second_out), (nu, nu_out)))]
-
-    def inner_out():
-        return pltpu.make_async_copy(lam.at[:, pl.ds(1, bx - 2)], out_ref.at[:, pl.ds(1, bx - 2)],
-                                     out_sem.at[4])
-
-    def edge_out(x, k):
-        return pltpu.make_async_copy(lam.at[:, pl.ds(x, 1)], out_ref.at[:, pl.ds(x, 1)],
-                                     out_sem.at[k])
-
     def update_tiles():
-        inner_out().start()
         wait_for(grads.at[pl.ds(1, n - 1)], all_got.at[2])
         rows = theta_ref.shape[0]
         pairs = n // 2
@@ -647,8 +635,6 @@
         first_new[...] = first
         second_new[...] = second
         theta_new[...] = theta_ref[...] - LEARN_RATE * first_hat / (jnp.sqrt(second_hat) + ADAM_EPS)
-        for copy in small_out:
-            copy.start()
 
     old, rim = pops.at[(STEPS - 1) % 2], rims.at[(STEPS - 1) % 2]
 
@@ -660,8 +646,6 @@
         return carry
 
     fed_step(end, 0, old, rim, ROUND_ADJ + STEPS - 1, opposite, between=update_tiles)
-    edge_out(0, 5).start()
-    edge_out(bx - 1, 6).start()
 
     wait_for(start.at[:, pl.ds(0, (n_st - 1) * planes)], check_sent)
     wait_for(flag_out, flag_sent)
@@ -671,17 +655,14 @@
     wait_for(tiles.at[pl.ds(1, n - 1)], all_sent.at[0])
     wait_for(heat.at[pl.ds(1, n - 1)], all_sent.at[1])
     wait_for(grads.at[pl.ds(1, n - 1)], all_sent.at[2])
-    for copy in small_out:
-        copy.wait()
-    inner_out().wait()
-    edge_out(0, 5).wait()
-    edge_out(bx - 1, 6).wait()
-
-
-def deliver(*refs):
-    sem = refs[-1]
-    half = (len(refs) - 1) // 2
-    copies = [pltpu.make_async_copy(refs[k], refs[half + k], sem.at[k]) for k in range(half)]
+
+
+def deliver(lam, theta_new, first_new, second_new, nu, lam_out, theta_out, first_out, second_out, nu_out,
+            scalar, sem):
+    scalar[...] = nu[0:1, 0:1]
+    pairs = ((lam, lam_out), (theta_new, theta_out), (first_new, first_out),
+             (second_new, second_out), (scalar, nu_out))
+    copies = [pltpu.make_async_copy(source, into, sem.at[k]) for k, (source, into) in enumerate(pairs)]
     for copy in copies:
         copy.start()
     for copy in copies:
@@ -703,17 +684,13 @@
               jax.ShapeDtypeStruct((1, 1), f32))
     results = pl.pallas_call(
         functools.partial(kernel, n_gx, n_st, planes),
-        out_shape=tuple(pltpu.HBM(value.shape, f32) for value in shapes),
+        out_shape=tuple(pltpu.VMEM(value.shape, f32) for value in shapes[:4]) + (
+            pltpu.VMEM((by, nz), f32),),
         in_specs=[hbm] * 7,
-        out_specs=(hbm,) * 5,
+        out_specs=(vmem,) * 5,
         scratch_shapes=[
             pltpu.VMEM((bx, by, nz), jnp.int32),
             pltpu.VMEM((bx, by), jnp.int32),
-            pltpu.VMEM((rows, nz), f32),
-            pltpu.VMEM((rows, nz), f32),
-            pltpu.VMEM((rows, nz), f32),
-            pltpu.VMEM((26, bx, by, nz), f32),
-            pltpu.VMEM((1, 1), f32),
             pltpu.VMEM((rows, nz), f32),
             pltpu.VMEM((rows, nz), f32),
             pltpu.VMEM((rows, nz), f32),
@@ -752,7 +729,6 @@
             dma,
             dma,
             dma((5,)),
-            dma((7,)),
         ],
         compiler_params=pltpu.CompilerParams(
             collective_id=0, has_side_effects=True, vmem_limit_bytes=40 * 1024 * 1024),
@@ -763,11 +739,11 @@
     adjoint_out, theta_new, first_new, second_new, nusselt = pl.pallas_call(
         deliver,
         out_shape=shapes,
-        in_specs=[hbm] * 5,
+        in_specs=[vmem] * 5,
         out_specs=(hbm,) * 5,
-        scratch_shapes=[dma((5,))],
+        scratch_shapes=[pltpu.VMEM((1, 1), f32), dma((5,))],
         name="deliver",
-    )(*(pltpu.with_memory_space_constraint(value, pltpu.HBM) for value in results))
+    )(*(pltpu.with_memory_space_constraint(value, pltpu.VMEM) for value in results))
     flat = theta.shape
     return (adjoint_out, theta_new.reshape(flat), first_new.reshape(flat),
             second_new.reshape(flat), nusselt.reshape(()))

time: 91.5 us -> 62.6 us (0.68)
  Pallas kernels: 90.7 us -> 61.8 us
    pallas_call x1, Pallas kernels: 29.1 us -> 0.96 us  [body(): pl.pallas_call(deliver, out_shape=shapes, in_specs=[vmem] * 5, out_specs=...]
where the time goes in v1:
time: 62.6 us; the launch traced here: 62.5 us
  Pallas kernels  61.8 us (99%)
  between operations  0.64 us (1%)
    pallas_call x1, Pallas kernels, body(): pl.pallas_call(functools.partial(kernel, n_gx, n_st, planes), out_shape=t...  60.9 us

profile of v1, /device:TPU:0, one launch (start us, length us, event | category | flops | bytes accessed | tf_op | source)
XLA Modules:
  0.0 62.5 jit_solution(9877262849818489098)
XLA Ops:
  0.6 60.9 %window.1 = (f32[26,8,8,128]{3,2,1,0:T(8,128)S(1)}, f32[32,128]{1,0:T(8,128)S(1)}, f32[32,128]{1,0:T(8,128)S(1)}, f32[32,128]{1,0:T(8,128)S(1)}, f32[8,128]{1,0:T(8,128)S(1)}) custom-call(f32[26,2,32,128]{3,2,1,0:T(8,128)} %check_ref.1, f32[26,8,8,128]{3,2,1,0:T(8,128)} %adj_ref.1, s32[8,8,128]{2,1,0:T(8,128)} %solid_hbm.1, s32[8,8]{1,0:T(8,128)} %map_hbm.1, ...), custom_call_target="tpu_custom_call" | custom-call | tf_op jit(solution)/shard_map/window/pallas_call | solution.py:685
  61.5 1.0 %deliver.1 = (f32[26,8,8,128]{3,2,1,0:T(8,128)}, f32[32,128]{1,0:T(8,128)}, f32[32,128]{1,0:T(8,128)}, f32[32,128]{1,0:T(8,128)}, f32[1,1]{1,0:T(1,128)}) custom-call(f32[26,8,8,128]{3,2,1,0:T(8,128)S(1)} %get-tuple-element.15.lam, f32[32,128]{1,0:T(8,128)S(1)} %get-tuple-element.16.theta_new, f32[32,128]{1,0:T(8,128)S(1)} %get-tuple-element.17.first_new, ...), custom_call_target="tpu_custom_call" | custom-call | tf_op jit(solution)/shard_map/deliver/pallas_call | solution.py:739
